TPU v7x, 512 devices: a whole 4x4x16 slice. The times are simulated.
512 devices in a mesh: gx: 64 (over x, z), gy: 8 (over y, core).
Axes of the slice: x: 4, y: 4, z: 16, core: 2. Of those that a mesh axis runs over, the one named last changes fastest.
Arguments:
- background: float32 [64, 256, 64, 128], P(None, 'gx', 'gy'), may hold values from -1.0358009 to 1.0358009
- sensor_cells: int32 [64], replicated, may hold values from 0 to 2097151
- sensor_gain: float32 [64], replicated, may hold values from 1 to 4
- center: float32 [256, 64, 128], P('gx', 'gy'), may hold values from 0.4 to 0.9
- neighbours: float32 [6, 256, 64, 128], P(None, 'gx', 'gy'), may hold values from 0.02 to 0.16
Outputs:
- modes: float32 [64, 256, 64, 128], P(None, 'gx', 'gy')
- r_factor: float32 [64, 64], replicated
- first_r: float32 [64, 64], replicated
All inputs are finite; a program needn't handle non-finite values.
Results may differ from a plain program's by a relative error of at most 0.0012.
Values sent between devices are 32-bit elements; how exact they have to be, the bound alone decides.
A program may use at most 64 MiB of HBM per device.

v0:
```python
import jax
import jax.numpy as jnp
from jax import lax
from jax.sharding import PartitionSpec as P


def with_halo(cells, sides, width):
    for axis, dim in sides:
        count = lax.axis_size(axis)
        ends = count - 1
        head = lax.slice_in_dim(cells, 0, width, axis=dim)
        tail = lax.slice_in_dim(cells, cells.shape[dim] - width, cells.shape[dim], axis=dim)
        cells = jnp.concatenate(
            [
                lax.ppermute(tail, axis, [(i, (i + 1) % count) for i in range(ends)]),
                cells,
                lax.ppermute(head, axis, [((i + 1) % count, i) for i in range(ends)]),
            ],
            axis=dim,
        )
    return cells


def advance(padded, center, neighbours):
    core = padded[..., 1:-1, 1:-1, :]
    widths = [(0, 0)] * (core.ndim - 1) + [(1, 1)]
    zpadded = jnp.pad(core, widths)
    result = center * core
    result = result + neighbours[0] * padded[..., 2:, 1:-1, :]
    result = result + neighbours[1] * padded[..., :-2, 1:-1, :]
    result = result + neighbours[2] * padded[..., 1:-1, 2:, :]
    result = result + neighbours[3] * padded[..., 1:-1, :-2, :]
    result = result + neighbours[4] * zpadded[..., 2:]
    result = result + neighbours[5] * zpadded[..., :-2]
    return result


def local(background, sensor_cells, sensor_gain, center, neighbours):
    count, width_x, width_y, depth_z = background.shape
    cells_y = width_y * lax.axis_size("gy")
    shape_local = (width_x, width_y, depth_z)
    along_x = lax.axis_index("gx") * width_x + lax.broadcasted_iota(jnp.int32, shape_local, 0)
    along_y = lax.axis_index("gy") * width_y + lax.broadcasted_iota(jnp.int32, shape_local, 1)
    along_z = lax.broadcasted_iota(jnp.int32, shape_local, 2)
    cell_ids = (along_x * cells_y + along_y) * depth_z + along_z
    at_sensor = cell_ids[None] == sensor_cells[:, None, None, None]
    adjoint = background + jnp.where(at_sensor, sensor_gain[:, None, None, None], 0.0)
    for repeat in range(2):
        padded = with_halo(adjoint, (("gx", 1), ("gy", 2)), 1)
        adjoint = advance(padded, center, neighbours)
    snapshot = adjoint.reshape(count, -1)
    gram_one = lax.psum(
        jnp.dot(snapshot, snapshot.T, precision=lax.Precision.HIGHEST), ("gx", "gy")
    )
    factor_one = jnp.linalg.cholesky(gram_one)
    basis_one = jax.scipy.linalg.solve_triangular(factor_one, snapshot, lower=True)
    gram_two = lax.psum(
        jnp.dot(basis_one, basis_one.T, precision=lax.Precision.HIGHEST), ("gx", "gy")
    )
    factor_two = jnp.linalg.cholesky(gram_two)
    basis_two = jax.scipy.linalg.solve_triangular(factor_two, basis_one, lower=True)
    upper = jnp.dot(factor_one, factor_two, precision=lax.Precision.HIGHEST).T
    total_cells = snapshot.shape[1] * lax.axis_size("gx") * lax.axis_size("gy")
    root_cells = jnp.sqrt(jnp.float32(total_cells))
    modes = (basis_two * root_cells).reshape(background.shape)
    return (modes, upper / root_cells, factor_one.T / root_cells)


def solution(mesh):
    in_specs = (P(None, "gx", "gy", None), P(), P(), P("gx", "gy", None), P(None, "gx", "gy", None))
    out_specs = (P(None, "gx", "gy", None), P(), P())
    return jax.shard_map(local, mesh=mesh, in_specs=in_specs, out_specs=out_specs, check_vma=False)
```

profile of v0, /device:TPU:1, one launch (start us, length us, event | category | flops | bytes accessed | tf_op | source)
XLA Modules:
  0.0 290.8 jit_solution(2853708214520666632)
XLA Ops:
  0.7 0.1 iota_add_fusion
  0.7 1.9 copy_add_fusion
  2.7 0.0 copy-start
  2.7 4.5 %collective-permute-start.1 = (f32[64,1,8,128]{3,0,2,1:T(8,128)S(1)}, f32[64,1,8,128]{3,0,2,1:T(8,128)S(1)}, u32[]{:S(2)}, u32[]{:S(2)}) collective-permute-start(f32[64,1,8,128]{3,0,2,1:T(8,128)S(1)} %get-tuple-element.20), channel_id=1, source_target_pairs={{0,8},{8,16},{16,24},{24,32},{32,40},{40,48},{48,56},{56,64},{64,7... | collective-permute-start | bytes 786440 | tf_op jit(solution)/shard_map/ppermute | solution.py:15
  7.2 0.0 copy-start.1
  7.2 1.3 collective-permute-start
  8.5 2.0 collective-permute-done.1
  10.5 4.0 %collective-permute-done = f32[64,1,8,128]{3,0,2,1:T(8,128)S(1)} collective-permute-done((f32[64,1,8,128]{3,0,2,1:T(8,128)S(1)}, f32[64,1,8,128]{3,0,2,1:T(8,128)S(1)}, u32[]{:S(2)}, u32[]{:S(2)}) %collective-permute-start) | collective-permute-done | bytes 262176 | tf_op jit(solution)/shard_map/ppermute | solution.py:17
  14.6 6.7 %collective-permute-start.2 = (f32[64,6,1,128]{3,0,2,1:T(8,128)S(1)}, f32[64,6,1,128]{3,0,2,1:T(8,128)S(1)}, u32[]{:S(2)}, u32[]{:S(2)}) collective-permute-start(f32[64,6,1,128]{3,0,2,1:T(8,128)S(1)} %get-tuple-element.16), channel_id=1, source_target_pairs={{1,0},{2,1},{3,2},{4,3},{5,4},{6,5},{7,6},{9,8},{10,9},{11,10},{12... | collective-permute-start | bytes 589832 | tf_op jit(solution)/shard_map/ppermute | solution.py:17
  21.3 1.9 collective-permute-start.3
  23.2 0.0 copy-done
  23.2 1.3 collective-permute-done.2
  24.5 1.3 collective-permute-done.3
  25.8 0.0 copy-done.1
  25.8 0.7 fusion.3
  26.5 3.5 %collective-permute-start.5 = (f32[64,1,8,128]{3,0,2,1:T(8,128)S(1)}, f32[64,1,8,128]{3,0,2,1:T(8,128)S(1)}, u32[]{:S(2)}, u32[]{:S(2)}) collective-permute-start(f32[64,1,8,128]{3,0,2,1:T(8,128)S(1)} %get-tuple-element.18), channel_id=1, source_target_pairs={{0,8},{8,16},{16,24},{24,32},{32,40},{40,48},{48,56},{56,64},{64,7... | collective-permute-start | bytes 786440 | tf_op jit(solution)/shard_map/ppermute | solution.py:15
  30.0 1.3 collective-permute-start.4
  31.3 3.0 %collective-permute-done.5 = f32[64,1,8,128]{3,0,2,1:T(8,128)S(1)} collective-permute-done((f32[64,1,8,128]{3,0,2,1:T(8,128)S(1)}, f32[64,1,8,128]{3,0,2,1:T(8,128)S(1)}, u32[]{:S(2)}, u32[]{:S(2)}) %collective-permute-start.5) | collective-permute-done | bytes 262176 | tf_op jit(solution)/shard_map/ppermute | solution.py:15
  34.3 5.2 %collective-permute-done.4 = f32[64,1,8,128]{3,0,2,1:T(8,128)S(1)} collective-permute-done((f32[64,1,8,128]{3,0,2,1:T(8,128)S(1)}, f32[64,1,8,128]{3,0,2,1:T(8,128)S(1)}, u32[]{:S(2)}, u32[]{:S(2)}) %collective-permute-start.4) | collective-permute-done | bytes 262176 | tf_op jit(solution)/shard_map/ppermute | solution.py:17
  39.5 1.9 collective-permute-start.6
  41.5 5.5 %collective-permute-start.7 = (f32[64,6,1,128]{3,0,2,1:T(8,128)S(1)}, f32[64,6,1,128]{3,0,2,1:T(8,128)S(1)}, u32[]{:S(2)}, u32[]{:S(2)}) collective-permute-start(f32[64,6,1,128]{3,0,2,1:T(8,128)S(1)} %get-tuple-element.15), channel_id=1, source_target_pairs={{0,1},{1,2},{2,3},{3,4},{4,5},{5,6},{6,7},{8,9},{9,10},{10,11},{11... | collective-permute-start | bytes 589832 | tf_op jit(solution)/shard_map/ppermute | solution.py:15
  47.0 1.4 collective-permute-done.6
  48.4 1.2 collective-permute-done.7
  49.6 0.7 fusion.7
  50.3 1.0 convolution_bitcast_fusion
  51.2 0.6 copy.24
  51.9 108.0 %psum.14 = f32[64,64]{0,1:T(8,128)S(1)} all-reduce(f32[64,64]{0,1:T(8,128)S(1)} %convolution_bitcast_fusion), channel_id=1, replica_groups=mesh['gx'=64,'gy'=8] {'gx','gy'}, use_global_device_ids=true, to_apply=%region_0.1 | all-reduce | flops 4096 | bytes 32768 | tf_op jit(solution)/shard_map/psum | solution.py:52
  159.8 0.1 copy.23
  159.9 5.8 %cholesky.44 = f32[64,64]{1,0:T(8,128)S(1)} custom-call(f32[64,64]{1,0:T(8,128)S(1)} %fusion.31), custom_call_target="Cholesky" | custom-call | tf_op jit(solution)/shard_map/jit(cholesky)/cholesky | solution.py:55
  165.8 0.6 compare_reduce_fusion.1
  166.5 0.7 multiply_bitcast_fusion
  167.1 4.9 %custom-call.6 = f32[1,64,64]{1,2,0:T(8,128)S(1)} custom-call(f32[1,64,64]{2,1,0:T(8,128)S(1)} %get-tuple-element.29), custom_call_target="InvertDiagBlocksLowerTriangular" | custom-call | tf_op jit(solution)/shard_map/jit(_solve_triangular)/triangular_solve | solution.py:56
  172.0 1.6 fusion.9
  173.6 1.0 fusion.48
  174.6 99.0 %psum.15 = f32[64,64]{0,1:T(8,128)S(1)} all-reduce(f32[64,64]{0,1:T(8,128)S(1)} %fusion.48), channel_id=1, replica_groups=mesh['gx'=64,'gy'=8] {'gx','gy'}, use_global_device_ids=true, to_apply=%region_3.6 | all-reduce | flops 4096 | bytes 32768 | tf_op jit(solution)/shard_map/psum | solution.py:57
  273.6 0.1 copy.26
  273.7 5.8 %cholesky.55 = f32[64,64]{1,0:T(8,128)S(1)} custom-call(f32[64,64]{1,0:T(8,128)S(1)} %fusion.29), custom_call_target="Cholesky" | custom-call | tf_op jit(solution)/shard_map/jit(cholesky)/cholesky | solution.py:60
  279.6 0.6 compare_reduce_fusion
  280.2 2.1 convolution_multiply_fusion.1
  282.4 0.7 select_bitcast_fusion
  283.0 0.7 copy.27
  283.7 4.9 %custom-call.7 = f32[1,64,64]{1,2,0:T(8,128)S(1)} custom-call(f32[1,64,64]{2,1,0:T(8,128)S(1)} %select_bitcast_fusion), custom_call_target="InvertDiagBlocksLowerTriangular" | custom-call | tf_op jit(solution)/shard_map/jit(_solve_triangular)/triangular_solve | solution.py:61
  288.6 1.1 fusion
  289.7 1.2 copy.32
  (11 shorter events, 0.2 us)
Async XLA Ops:
  2.7 20.5 %copy-start = (f32[6,4,8,128]{3,2,1,0:T(8,128)S(1)}, f32[6,4,8,128]{3,2,1,0:T(8,128)}, u32[]{:S(2)}) copy-start(f32[6,4,8,128]{3,2,1,0:T(8,128)} %param.12) | copy-start | bytes 294916
  2.7 7.8 %collective-permute-start.1 = (f32[64,1,8,128]{3,0,2,1:T(8,128)S(1)}, f32[64,1,8,128]{3,0,2,1:T(8,128)S(1)}, u32[]{:S(2)}, u32[]{:S(2)}) collective-permute-start(f32[64,1,8,128]{3,0,2,1:T(8,128)S(1)} %get-tuple-element.20), channel_id=1, source_target_pairs={{0,8},{8,16},{16,24},{24,32},{32,40},{40,48},{48,56},{56,64},{64,7... | collective-permute-start | bytes 786440 | tf_op jit(solution)/shard_map/ppermute | solution.py:15
  7.2 18.5 %copy-start.1 = (f32[4,8,128]{2,1,0:T(8,128)S(1)}, f32[4,8,128]{2,1,0:T(8,128)}, u32[]{:S(2)}) copy-start(f32[4,8,128]{2,1,0:T(8,128)} %param.11) | copy-start | bytes 49156
  7.2 7.3 %collective-permute-start = (f32[64,1,8,128]{3,0,2,1:T(8,128)S(1)}, f32[64,1,8,128]{3,0,2,1:T(8,128)S(1)}, u32[]{:S(2)}, u32[]{:S(2)}) collective-permute-start(f32[64,1,8,128]{3,0,2,1:T(8,128)S(1)} %get-tuple-element.21), channel_id=1, source_target_pairs={{8,0},{16,8},{24,16},{32,24},{40,32},{48,40},{56,48},{64,56},{72,6... | collective-permute-start | bytes 786440 | tf_op jit(solution)/shard_map/ppermute | solution.py:17
  14.6 9.9 %collective-permute-start.2 = (f32[64,6,1,128]{3,0,2,1:T(8,128)S(1)}, f32[64,6,1,128]{3,0,2,1:T(8,128)S(1)}, u32[]{:S(2)}, u32[]{:S(2)}) collective-permute-start(f32[64,6,1,128]{3,0,2,1:T(8,128)S(1)} %get-tuple-element.16), channel_id=1, source_target_pairs={{1,0},{2,1},{3,2},{4,3},{5,4},{6,5},{7,6},{9,8},{10,9},{11,10},{12... | collective-permute-start | bytes 589832 | tf_op jit(solution)/shard_map/ppermute | solution.py:17
  21.3 4.5 %collective-permute-start.3 = (f32[64,6,1,128]{3,0,2,1:T(8,128)S(1)}, f32[64,6,1,128]{3,0,2,1:T(8,128)S(1)}, u32[]{:S(2)}, u32[]{:S(2)}) collective-permute-start(f32[64,6,1,128]{3,0,2,1:T(8,128)S(1)} %get-tuple-element.17), channel_id=1, source_target_pairs={{0,1},{1,2},{2,3},{3,4},{4,5},{5,6},{6,7},{8,9},{9,10},{10,11},{11... | collective-permute-start | bytes 589832 | tf_op jit(solution)/shard_map/ppermute | solution.py:15
  26.5 7.8 %collective-permute-start.5 = (f32[64,1,8,128]{3,0,2,1:T(8,128)S(1)}, f32[64,1,8,128]{3,0,2,1:T(8,128)S(1)}, u32[]{:S(2)}, u32[]{:S(2)}) collective-permute-start(f32[64,1,8,128]{3,0,2,1:T(8,128)S(1)} %get-tuple-element.18), channel_id=1, source_target_pairs={{0,8},{8,16},{16,24},{24,32},{32,40},{40,48},{48,56},{56,64},{64,7... | collective-permute-start | bytes 786440 | tf_op jit(solution)/shard_map/ppermute | solution.py:15
  30.0 9.5 %collective-permute-start.4 = (f32[64,1,8,128]{3,0,2,1:T(8,128)S(1)}, f32[64,1,8,128]{3,0,2,1:T(8,128)S(1)}, u32[]{:S(2)}, u32[]{:S(2)}) collective-permute-start(f32[64,1,8,128]{3,0,2,1:T(8,128)S(1)} %get-tuple-element.19), channel_id=1, source_target_pairs={{8,0},{16,8},{24,16},{32,24},{40,32},{48,40},{56,48},{64,56},{72,6... | collective-permute-start | bytes 786440 | tf_op jit(solution)/shard_map/ppermute | solution.py:17
  39.5 8.9 %collective-permute-start.6 = (f32[64,6,1,128]{3,0,2,1:T(8,128)S(1)}, f32[64,6,1,128]{3,0,2,1:T(8,128)S(1)}, u32[]{:S(2)}, u32[]{:S(2)}) collective-permute-start(f32[64,6,1,128]{3,0,2,1:T(8,128)S(1)} %get-tuple-element.14), channel_id=1, source_target_pairs={{1,0},{2,1},{3,2},{4,3},{5,4},{6,5},{7,6},{9,8},{10,9},{11,10},{12... | collective-permute-start | bytes 589832 | tf_op jit(solution)/shard_map/ppermute | solution.py:17
  41.5 8.1 %collective-permute-start.7 = (f32[64,6,1,128]{3,0,2,1:T(8,128)S(1)}, f32[64,6,1,128]{3,0,2,1:T(8,128)S(1)}, u32[]{:S(2)}, u32[]{:S(2)}) collective-permute-start(f32[64,6,1,128]{3,0,2,1:T(8,128)S(1)} %get-tuple-element.15), channel_id=1, source_target_pairs={{0,1},{1,2},{2,3},{3,4},{4,5},{5,6},{6,7},{8,9},{9,10},{10,11},{11... | collective-permute-start | bytes 589832 | tf_op jit(solution)/shard_map/ppermute | solution.py:15
where the time goes:
time: 292 us; the launch traced here: 291 us
  blocking collectives  207 us (71%)
  other arithmetic  27.5 us (9%)
  starting transfers between devices  26.6 us (9%)
  waiting for transfers between devices  19.4 us (7%)
  matrix products  6.74 us (2%)
    psum x1, blocking collectives, local(): lax.psum(jnp.dot(snapshot, snapshot.T, precision=lax.Precision.HIGHEST),...  108 us
    psum x1, blocking collectives, local(): lax.psum(jnp.dot(basis_one, basis_one.T, precision=lax.Precision.HIGHEST)...  99 us
    ppermute x4, starting transfers between devices, with_halo(): lax.ppermute(tail, axis, [(i, (i + 1) % count) for i in range(ends)])  15.4 us
    ppermute x4, waiting for transfers between devices, with_halo(): lax.ppermute(head, axis, [((i + 1) % count, i) for i in range(ends)])  11.9 us
    ppermute x4, starting transfers between devices, with_halo(): lax.ppermute(head, axis, [((i + 1) % count, i) for i in range(ends)])  11.2 us
    ppermute x4, waiting for transfers between devices, with_halo(): lax.ppermute(tail, axis, [(i, (i + 1) % count) for i in range(ends)])  7.45 us
    another operation x3, other arithmetic, local(): factor_one = jnp.linalg.cholesky(gram_one)  6.52 us
    another operation x3, other arithmetic, local(): factor_two = jnp.linalg.cholesky(gram_two)  6.52 us
  transfers between devices with their start and end apart: 8, of which 8 were waited for; matrix products, arithmetic and copies ran while one was open for 0% of the time, Pallas kernels for 0%

commit v1 on v0

v1 whole, which is shorter than its diff:
```python
import functools

import jax
import jax.numpy as jnp
from jax import lax
from jax.experimental import pallas as pl
from jax.experimental.pallas import tpu as pltpu
from jax.sharding import PartitionSpec as P

MESH = pl.DeviceIdType.MESH
F32 = jnp.float32
HIGHEST = lax.Precision.HIGHEST
ROW_CHUNKS = (0, 3, 1, 2)


def two_sum(a, b):
    s = a + b
    t = s - a
    return s, (a - (s - t)) + (b - t)


def power_below(m):
    q = m * F32(8388609.0)
    return jnp.abs(q - q * F32(0.99999994))


def pieces(s, big):
    first = (s + big) - big
    rest = s - first
    small = big * F32(1.0 / 256)
    second = (rest + small) - small
    return first, second, rest - second


def outer_sums(stacked):
    n = stacked.shape[0] // 3
    prod = lax.dot_general(stacked, stacked, (((1,), (1,)), ((), ())), preferred_element_type=F32)
    b = [[prod[i * n : (i + 1) * n, j * n : (j + 1) * n] for j in range(3)] for i in range(3)]
    mid, e1 = two_sum(b[0][1], b[1][0])
    high, e2 = two_sum(b[0][0], mid)
    low = ((b[0][2] + b[2][0]) + b[1][1]) + (b[1][2] + b[2][1]) + (e1 + e2)
    return high, low


class Group:
    def __init__(self, axis, digits):
        self.axis, self.digits = axis, digits
        self.size = 1
        for _, count in digits:
            self.size *= count

    def rank(self):
        me = lax.axis_index(self.axis)
        rank = 0
        for stride, count in self.digits:
            rank = rank * count + (me // stride) % count
        return rank

    def member(self, rank):
        me = lax.axis_index(self.axis)
        index = me
        for stride, count in reversed(self.digits):
            index = index + (rank % count - (me // stride) % count) * stride
            rank = rank // count
        return index


def groups_of(size_x):
    if size_x == 64:
        return [Group("gx", [(16, 4), (1, 2)]), Group("gx", [(2, 8)])]
    half = size_x // 2
    return [Group("gx", [(1, 2)]), Group("gx", [(2, half)])]


def sum_slots(buf, count, lanes):
    def body(i, carry):
        total, err = carry
        total, e = two_sum(total, buf[i])
        return total, err + e

    total, err = buf[0], jnp.zeros_like(buf[0])
    for i in range(1, count):
        total, err = body(i, (total, err))
    half = lanes // 2
    low = err + pltpu.roll(total, half, 1)
    high = total + low
    low = low - (high - total)
    lane = lax.broadcasted_iota(jnp.int32, high.shape, 1)
    return jnp.where(lane < half, high, pltpu.roll(low, half, 1))


def fields_kernel(
    nx, ny, cells_ref, gain_ref, bg_ref, cen_ref, nei_ref, s_out, g_out,
    bg_v, v_ref, w_ref, s_ref, rel_ref, gains_ref, xs_ref, pack_ref, piece_ref, buf0, buf1, buf2,
    load_sem, store_sem, x_send, x_recv, y_send, y_recv, r_send, r_recv,
):
    gx, gy = lax.axis_index("gx"), lax.axis_index("gy")
    width_x, width_y, k, lanes = 4, 8, v_ref.shape[2], v_ref.shape[3]
    y_group = Group("gy", [(1, ny)])
    groups = groups_of(nx)
    has_left, has_right = gx > 0, gx < nx - 1
    has_down, has_up = gy > 0, gy < ny - 1

    load = pltpu.make_async_copy(bg_ref, bg_v, load_sem)
    load.start()

    barrier = pltpu.get_barrier_semaphore()
    expected = 0
    for group in [y_group] + groups:
        rank = group.rank()
        for step in range(1, group.size):
            to = group.member((rank + step) % group.size)
            pl.semaphore_signal(barrier, inc=1, device_id={group.axis: to}, device_id_type=MESH)
            expected += 1

    @pl.when(has_left)
    def _():
        pl.semaphore_signal(barrier, inc=1, device_id={"gx": gx - 1}, device_id_type=MESH)

    @pl.when(has_right)
    def _():
        pl.semaphore_signal(barrier, inc=1, device_id={"gx": gx + 1}, device_id_type=MESH)

    zero_plane = jnp.zeros((width_y, k, lanes), F32)
    for edge, row in ((~has_left, 0), (~has_right, width_x + 1)):
        @pl.when(edge)
        def _(row=row):
            v_ref[row, 1 : width_y + 1] = zero_plane
            w_ref[row, 1 : width_y + 1] = zero_plane

    for edge, row in ((~has_down, 0), (~has_up, width_y + 1)):
        @pl.when(edge)
        def _(row=row):
            v_ref[1 : width_x + 1, row] = jnp.zeros((width_x, k, lanes), F32)
            w_ref[1 : width_x + 1, row] = jnp.zeros((width_x, k, lanes), F32)

    sub = lax.broadcasted_iota(jnp.int32, (k, lanes), 0)
    lane = lax.broadcasted_iota(jnp.int32, (k, lanes), 1)

    def spread(i, carry):
        cells, gains = carry
        here = sub == i
        return jnp.where(here, cells_ref[i], cells), jnp.where(here, gain_ref[i], gains)

    cells, gains = lax.fori_loop(0, k, spread, (jnp.zeros((k, lanes), jnp.int32), jnp.zeros((k, lanes), F32)))
    rel_ref[...] = cells - lane
    gains_ref[...] = gains

    load.wait()

    def take(i, _):
        x, y = i // width_y, i % width_y
        at = ((gx * width_x + x) * (width_y * ny) + gy * width_y + y) * lanes
        rows = bg_v[pl.ds(i, k, stride=width_x * width_y), :]
        v_ref[x + 1, y + 1] = rows + jnp.where(rel_ref[...] == at, gains_ref[...], 0.0)
        return 0

    lax.fori_loop(0, width_x * width_y, take, 0)
    pl.semaphore_wait(barrier, expected + has_left.astype(jnp.int32) + has_right.astype(jnp.int32))

    def x_copy(buf, which, c, side):
        rows = pl.ds(1 + 2 * c, 2)
        source, target = ((1, width_x + 1), (width_x, 0))[side]
        return pltpu.make_async_remote_copy(
            src_ref=buf.at[source, rows], dst_ref=buf.at[target, rows],
            send_sem=x_send.at[which, side, c], recv_sem=x_recv.at[which, side, c],
            device_id={"gx": (gx - 1, gx + 1)[side]}, device_id_type=MESH,
        )

    def y_copy(buf, which, side):
        source, target = ((1, width_y + 1), (width_y, 0))[side]
        planes = pl.ds(1, width_x)
        return pltpu.make_async_remote_copy(
            src_ref=buf.at[planes, source], dst_ref=buf.at[planes, target],
            send_sem=y_send.at[which, side], recv_sem=y_recv.at[which, side],
            device_id={"gy": (gy - 1, gy + 1)[side]}, device_id_type=MESH,
        )

    there_x, there_y = (has_left, has_right), (has_down, has_up)

    def start_x(buf, which, c):
        for side in (0, 1):
            @pl.when(there_x[side])
            def _(side=side):
                x_copy(buf, which, c, side).start()

    def start_y(buf, which, side):
        @pl.when(there_y[side])
        def _():
            y_copy(buf, which, side).start()

    def arrive_x(buf, which, c):
        for side in (0, 1):
            @pl.when(there_x[1 - side])
            def _(side=side):
                x_copy(buf, which, c, side).wait_recv()

    def arrive_y(buf, which, side):
        @pl.when(there_y[1 - side])
        def _():
            y_copy(buf, which, side).wait_recv()

    start_y(v_ref, 0, 0)
    start_y(v_ref, 0, 1)
    for c in ROW_CHUNKS:
        start_x(v_ref, 0, c)

    z_lane = lax.broadcasted_iota(jnp.int32, (1, lanes), 1)

    def advance(src, x, y):
        def row(ref):
            return jnp.broadcast_to(ref, (k, lanes))

        i = x * width_y + y
        core = src[x + 1, y + 1]
        upper = jnp.where(z_lane < lanes - 1, nei_ref[4, pl.ds(i, 1), :], 0.0)
        lower = jnp.where(z_lane > 0, nei_ref[5, pl.ds(i, 1), :], 0.0)
        result = row(cen_ref[pl.ds(i, 1), :]) * core
        result = result + row(nei_ref[0, pl.ds(i, 1), :]) * src[x + 2, y + 1]
        result = result + row(nei_ref[1, pl.ds(i, 1), :]) * src[x, y + 1]
        result = result + row(nei_ref[2, pl.ds(i, 1), :]) * src[x + 1, y + 2]
        result = result + row(nei_ref[3, pl.ds(i, 1), :]) * src[x + 1, y]
        result = result + row(upper) * pltpu.roll(core, lanes - 1, 1)
        result = result + row(lower) * pltpu.roll(core, 1, 1)
        return result

    arrive_y(v_ref, 0, 0)
    arrive_y(v_ref, 0, 1)
    for c in ROW_CHUNKS:
        arrive_x(v_ref, 0, c)

        def first(i, _, c=c):
            x, y = i // 2, 2 * c + i % 2
            w_ref[x + 1, y + 1] = advance(v_ref, x, y)
            return 0

        lax.fori_loop(0, 2 * width_x, first, 0)
        start_x(w_ref, 1, c)
        if c == 0:
            start_y(w_ref, 1, 0)
        if c == width_y // 2 - 1:
            start_y(w_ref, 1, 1)

    high = jnp.zeros((k, k), F32)
    low = jnp.zeros((k, k), F32)
    for turn, c in enumerate(ROW_CHUNKS):
        arrive_x(w_ref, 1, c)
        if c == 0:
            arrive_y(w_ref, 1, 1)
        if c == width_y // 2 - 1:
            arrive_y(w_ref, 1, 0)

        def second(i, most, c=c):
            x, y = i // 2, 2 * c + i % 2
            value = advance(w_ref, x, y)
            s_ref[c * 2 * width_x + i] = value
            return jnp.maximum(most, jnp.abs(value))

        most = lax.fori_loop(0, 2 * width_x, second, jnp.zeros((k, lanes), F32))
        part = pl.ds(c * 2 * width_x, 2 * width_x)
        pltpu.make_async_copy(s_ref.at[part], s_out.at[part], store_sem.at[c]).start()
        big = power_below(jnp.max(most, axis=1, keepdims=True)) * F32(1.5 * 2**17)
        for i in range(2 * width_x):
            for j, piece in enumerate(pieces(s_ref[c * 2 * width_x + i], big)):
                xs_ref[turn % 2, j * k : (j + 1) * k, i * lanes : (i + 1) * lanes] = piece.astype(jnp.bfloat16)
        part_high, part_low = outer_sums(xs_ref[turn % 2])
        high, e = two_sum(high, part_high)
        low = low + (part_low + e)

    pack_ref[...] = jnp.concatenate([high, low], axis=1)

    rows = k // ny
    y_rank = y_group.rank()

    def share(phase, group, source, target, slot, sem_slot):
        rank = group.rank()
        copies = []
        for step in range(1, group.size):
            peer = (rank + step) % group.size
            copies.append(pltpu.make_async_remote_copy(
                src_ref=source(peer), dst_ref=target(rank),
                send_sem=r_send.at[phase, step], recv_sem=r_recv.at[phase, rank],
                device_id={group.axis: group.member(peer)}, device_id_type=MESH,
            ))
        for copy in copies:
            copy.start()
        return copies

    def gather(phase, group, source, target):
        rank = group.rank()
        for step in range(1, group.size):
            peer = (rank + step) % group.size
            pltpu.make_async_remote_copy(
                src_ref=source(peer), dst_ref=target(peer),
                send_sem=r_send.at[phase, step], recv_sem=r_recv.at[phase, peer],
                device_id={group.axis: group.member(peer)}, device_id_type=MESH,
            ).wait_recv()

    sent = []

    def part_of(peer):
        return pack_ref.at[pl.ds(pl.multiple_of(peer * rows, rows), rows)]

    buf0[y_rank] = pack_ref[pl.ds(pl.multiple_of(y_rank * rows, rows), rows)]
    sent += share(0, y_group, part_of, lambda r: buf0.at[r], None, None)
    gather(0, y_group, part_of, lambda r: buf0.at[r])
    total = sum_slots(buf0, ny, lanes)
    for phase, (group, buf) in enumerate(zip(groups, (buf1, buf2)), 1):
        here = piece_ref.at[phase - 1]
        here[...] = total
        buf[group.rank()] = total
        sent += share(phase, group, lambda p: here, lambda r: buf.at[r], None, None)
        gather(phase, group, lambda p: here, lambda r: buf.at[r])
        total = sum_slots(buf, group.size, lanes)
    last = piece_ref.at[2]
    last[...] = total

    def rows_of(r):
        return g_out.at[pl.ds(pl.multiple_of(r * rows, rows), rows)]

    g_out[pl.ds(pl.multiple_of(y_rank * rows, rows), rows)] = total
    sent += share(3, y_group, lambda p: last, rows_of, None, None)
    gather(3, y_group, lambda p: last, rows_of)

    for copy in sent:
        copy.wait_send()
    for c in ROW_CHUNKS:
        part = pl.ds(c * 2 * width_x, 2 * width_x)
        pltpu.make_async_copy(s_ref.at[part], s_out.at[part], store_sem.at[c]).wait()
        for which, buf in enumerate((v_ref, w_ref)):
            for side in (0, 1):
                @pl.when(there_x[side])
                def _(c=c, which=which, buf=buf, side=side):
                    x_copy(buf, which, c, side).wait_send()
    for which, buf in enumerate((v_ref, w_ref)):
        for side in (0, 1):
            @pl.when(there_y[side])
            def _(which=which, buf=buf, side=side):
                y_copy(buf, which, side).wait_send()


def eliminate(a):
    n = a.shape[0]
    blocks = [a[8 * i : 8 * i + 8] for i in range(n // 8)]
    sub = lax.broadcasted_iota(jnp.int32, (8, 1), 0)
    for j in range(n):
        jb, jr = j // 8, j % 8
        row = blocks[jb][jr : jr + 1]
        scale = lax.rsqrt(row[:, j : j + 1])
        row = row * scale
        for i in range(jb, n // 8):
            update = (blocks[i][:, j : j + 1] * scale) * row
            if i == jb:
                blocks[i] = jnp.where(sub > jr, blocks[i] - update, jnp.where(sub == jr, row, blocks[i]))
            else:
                blocks[i] = blocks[i] - update
    return jnp.concatenate(blocks, axis=0)


def eye_mask(rows, columns):
    return lax.broadcasted_iota(jnp.int32, (rows, columns), 0) == lax.broadcasted_iota(jnp.int32, (rows, columns), 1)


def dot(a, b):
    return jnp.dot(a, b, precision=HIGHEST, preferred_element_type=F32)


def basis_kernel(root, s_hbm, g_ref, modes_ref, r_ref, first_ref, s_v, load_sem):
    k = g_ref.shape[0]
    load = pltpu.make_async_copy(s_hbm, s_v, load_sem)
    load.start()
    high, low = g_ref[:, :k], g_ref[:, k:]
    eye = eye_mask(k, k).astype(F32)
    row, column = lax.broadcasted_iota(jnp.int32, (k, k), 0), lax.broadcasted_iota(jnp.int32, (k, k), 1)
    upper = row <= column

    done = eliminate(jnp.concatenate([high, eye], axis=1))
    first = jnp.where(upper, done[:, :k], 0.0).T
    big = power_below(jnp.max(jnp.abs(first), axis=1, keepdims=True)) * F32(1.5 * 2**17)
    parts = [p.astype(jnp.bfloat16) for p in pieces(first, big)]
    first = (parts[2].astype(F32) + parts[1].astype(F32)) + parts[0].astype(F32)
    inverse = done[:, k:]
    full, rest = outer_sums(jnp.concatenate(parts, axis=0))
    left = (high - full) + (low - rest)
    gram = eye + dot(dot(inverse, left), inverse.T)

    done = eliminate(jnp.concatenate([gram, eye], axis=1))
    second_t = jnp.where(upper, done[:, :k], 0.0)
    weights = dot(done[:, k:], inverse) * root
    r_ref[...] = dot(second_t, first.T) * (1.0 / root)
    first_ref[...] = first.T * (1.0 / root)
    load.wait()
    count = s_v.shape[0]

    def body(i, _):
        x, y = i // 2 % (count // 8), i // (count // 4) * 2 + i % 2
        modes_ref[pl.ds(x * 8 + y, k, stride=count), :] = dot(weights, s_v[i])
        return 0

    lax.fori_loop(0, count, body, 0)


def local(nx, ny, background, sensor_cells, sensor_gain, center, neighbours):
    k, width_x, width_y, lanes = background.shape
    cells = width_x * width_y
    groups = groups_of(nx)
    vmem = pl.BlockSpec(memory_space=pltpu.VMEM)
    smem = pl.BlockSpec(memory_space=pltpu.SMEM)
    dma = pltpu.SemaphoreType.DMA
    slots = max([ny] + [g.size for g in groups])
    rows = k // ny
    fields, gram = pl.pallas_call(
        functools.partial(fields_kernel, nx, ny),
        out_shape=(jax.ShapeDtypeStruct((cells, k, lanes), F32), jax.ShapeDtypeStruct((k, 2 * k), F32)),
        in_specs=[smem, smem, pl.BlockSpec(memory_space=pl.ANY), vmem, vmem],
        out_specs=(pl.BlockSpec(memory_space=pl.ANY), vmem),
        scratch_shapes=[
            pltpu.VMEM((k * cells, lanes), F32),
            pltpu.VMEM((width_x + 2, width_y + 2, k, lanes), F32),
            pltpu.VMEM((width_x + 2, width_y + 2, k, lanes), F32),
            pltpu.VMEM((cells, k, lanes), F32),
            pltpu.VMEM((k, lanes), jnp.int32),
            pltpu.VMEM((k, lanes), F32),
            pltpu.VMEM((2, 3 * k, 2 * width_x * lanes), jnp.bfloat16),
            pltpu.VMEM((k, 2 * k), F32),
            pltpu.VMEM((3, rows, 2 * k), F32),
            pltpu.VMEM((ny, rows, 2 * k), F32),
            pltpu.VMEM((groups[0].size, rows, 2 * k), F32),
            pltpu.VMEM((groups[1].size, rows, 2 * k), F32),
            dma, dma((4,)),
            dma((2, 2, 4)), dma((2, 2, 4)), dma((2, 2)), dma((2, 2)),
            dma((4, slots)), dma((4, slots)),
        ],
        compiler_params=pltpu.CompilerParams(
            collective_id=0, has_side_effects=True, vmem_limit_bytes=24 * 2**20
        ),
        name="fields_and_products",
    )(
        sensor_cells, sensor_gain, background.reshape(k * cells, lanes),
        center.reshape(cells, lanes), neighbours.reshape(6, cells, lanes),
    )
    total_cells = cells * lanes * nx * ny
    root = float(total_cells) ** 0.5
    modes, r_factor, first_r = pl.pallas_call(
        functools.partial(basis_kernel, root),
        out_shape=(
            jax.ShapeDtypeStruct((k * cells, lanes), F32),
            jax.ShapeDtypeStruct((k, k), F32),
            jax.ShapeDtypeStruct((k, k), F32),
        ),
        in_specs=[pl.BlockSpec(memory_space=pl.ANY), vmem],
        out_specs=(vmem, vmem, vmem),
        scratch_shapes=[pltpu.VMEM((cells, k, lanes), F32), dma],
        compiler_params=pltpu.CompilerParams(vmem_limit_bytes=24 * 2**20),
        name="basis",
    )(fields, gram)
    return modes.reshape(background.shape), r_factor, first_r


def solution(mesh):
    nx, ny = mesh.shape["gx"], mesh.shape["gy"]
    in_specs = (P(None, "gx", "gy", None), P(), P(), P("gx", "gy", None), P(None, "gx", "gy", None))
    out_specs = (P(None, "gx", "gy", None), P(), P())
    return jax.shard_map(
        functools.partial(local, nx, ny), mesh=mesh, in_specs=in_specs, out_specs=out_specs, check_vma=False
    )
```

time: 292 us -> 77.6 us (0.27)
  blocking collectives: 207 us -> 0 us
  Pallas kernels: 0 us -> 73.2 us
  other arithmetic: 27.5 us -> 0 us
  starting transfers between devices: 26.6 us -> 0 us
  waiting for transfers between devices: 19.4 us -> 0 us
  matrix products: 6.74 us -> 0 us
    psum x2 -> x0, blocking collectives: 207 us -> none  [the longest x1 108 us: local(): lax.psum(jnp.dot(snapshot, snapshot.T, precision=lax.Precision.HIGHEST),...]
    pallas_call x0 -> x2, Pallas kernels: none -> 73.2 us  [the longest x1 54 us: local(): pl.pallas_call(functools.partial(fields_kernel, nx, ny), out_shape=(jax.S...]
    ppermute x8 -> x0, starting transfers between devices: 26.6 us -> none  [the longest x4 15.4 us: with_halo(): lax.ppermute(tail, axis, [(i, (i + 1) % count) for i in range(ends)])]
    another operation x9 -> x0, other arithmetic: 23.5 us -> none  [the longest x3 6.52 us: local(): factor_one = jnp.linalg.cholesky(gram_one)]
    ppermute x8 -> x0, waiting for transfers between devices: 19.4 us -> none  [the longest x4 11.9 us: with_halo(): lax.ppermute(head, axis, [((i + 1) % count, i) for i in range(ends)])]
    dot_general x3 -> x0, matrix products: 4.08 us -> none  [the longest x1 2.14 us: local(): upper = jnp.dot(factor_one, factor_two, precision=lax.Precision.HIGHEST).T]
    add x5 -> x0, other arithmetic: 3.3 us -> none  [the longest x1 1.9 us: local(): background + jnp.where(at_sensor, sensor_gain[:, None, None, None], 0.0)]
  transfers between devices with their start and end apart: 8 -> 0, of which waited for: 8 -> 0; matrix products, arithmetic and copies ran while one was open for 0% -> 0% of each run, Pallas kernels for 0% -> 0%
where the time goes in v1:
time: 77.6 us; the launch traced here: 77.4 us
  Pallas kernels  73.2 us (94%)
  local copies, waits for them, and re-layouts  3.49 us (4%)
    pallas_call x1, Pallas kernels, local(): pl.pallas_call(functools.partial(fields_kernel, nx, ny), out_shape=(jax.S...  54 us
    pallas_call x1, Pallas kernels, local(): pl.pallas_call(functools.partial(basis_kernel, root), out_shape=(jax.Shap...  19.2 us
    unnamed x10, local copies, waits for them, and re-layouts  3.49 us

profile of v1, /device:TPU:1, one launch (start us, length us, event | category | flops | bytes accessed | tf_op | source)
XLA Modules:
  0.0 77.4 jit_solution(15806785077753218547)
XLA Ops:
  0.6 0.0 copy-start.3
  0.6 0.0 copy-start.4
  0.7 0.6 copy-done.3
  1.3 0.0 copy-done.4
  1.3 0.0 copy-start
  1.3 1.2 %copy-done = f32[64,4,8,128]{3,2,1,0:T(8,128)S(1)} copy-done((f32[64,4,8,128]{3,2,1,0:T(8,128)S(1)}, f32[64,4,8,128]{3,2,1,0:T(8,128)}, u32[]{:S(2)}) %copy-start) | copy-done | bytes 1048600
  2.5 0.0 copy-start.1
  2.5 0.9 %copy-done.1 = f32[6,4,8,128]{3,2,1,0:T(8,128)S(1)} copy-done((f32[6,4,8,128]{3,2,1,0:T(8,128)S(1)}, f32[6,4,8,128]{3,2,1,0:T(8,128)}, u32[]{:S(2)}) %copy-start.1) | copy-done | bytes 98328
  3.4 0.0 copy-start.2
  3.4 0.7 copy-done.2
  4.1 54.0 %fields_and_products.1 = (f32[32,64,128]{2,1,0:T(8,128)S(1)}, f32[64,128]{1,0:T(8,128)S(1)}) custom-call(s32[64]{0:T(128)S(1)} %copy-done.3, f32[64]{0:T(128)S(1)} %copy-done.4, f32[2048,128]{1,0:T(8,128)S(1)} %bitcast.4, f32[32,128]{1,0:T(8,128)S(1)} %bitcast.6, f32[6,32,128]{2,1,0:T(8,128)S(1)} %bitcast.5), custom_call_target="tpu_custom_call" | custom-call | tf_op jit(solution)/shard_map/fields_and_products/pallas_call | solution.py:412
  58.1 19.2 %basis.1 = (f32[2048,128]{1,0:T(8,128)}, f32[64,64]{1,0:T(8,128)}, f32[64,64]{1,0:T(8,128)}) custom-call(f32[32,64,128]{2,1,0:T(8,128)S(1)} %get-tuple-element.8.s_hbm, f32[64,128]{1,0:T(8,128)S(1)} %get-tuple-element.9.g_ref), custom_call_target="tpu_custom_call" | custom-call | tf_op jit(solution)/shard_map/basis/pallas_call | solution.py:444
Async XLA Ops:
  0.6 0.7 copy-start.3
  0.6 0.7 copy-start.4
  1.3 1.2 %copy-start = (f32[64,4,8,128]{3,2,1,0:T(8,128)S(1)}, f32[64,4,8,128]{3,2,1,0:T(8,128)}, u32[]{:S(2)}) copy-start(f32[64,4,8,128]{3,2,1,0:T(8,128)} %param.5) | copy-start | bytes 3145732
  2.5 0.9 %copy-start.1 = (f32[6,4,8,128]{3,2,1,0:T(8,128)S(1)}, f32[6,4,8,128]{3,2,1,0:T(8,128)}, u32[]{:S(2)}) copy-start(f32[6,4,8,128]{3,2,1,0:T(8,128)} %param.9) | copy-start | bytes 294916
  3.4 0.7 copy-start.2

commit v2 on v1

--- a/solution.py
+++ b/solution.py
@@ -30,6 +30,11 @@
     small = big * F32(1.0 / 256)
     second = (rest + small) - small
     return first, second, rest - second
+
+
+def cut(a):
+    big = power_below(jnp.max(jnp.abs(a), axis=1, keepdims=True)) * F32(1.5 * 2**17)
+    return [p.astype(jnp.bfloat16) for p in pieces(a, big)]
 
 
 def outer_sums(stacked):
@@ -90,8 +95,8 @@
 
 
 def fields_kernel(
-    nx, ny, cells_ref, gain_ref, bg_ref, cen_ref, nei_ref, s_out, g_out,
-    bg_v, v_ref, w_ref, s_ref, rel_ref, gains_ref, xs_ref, pack_ref, piece_ref, buf0, buf1, buf2,
+    nx, ny, cells_hbm, gain_hbm, bg_ref, cen_hbm, nei_hbm, xs_out, g_out,
+    cells_ref, gain_ref, cen_ref, nei_ref, bg_v, v_ref, w_ref, s_ref, rel_ref, gains_ref, xs_ref, pack_ref, piece_ref, buf0, buf1, buf2,
     load_sem, store_sem, x_send, x_recv, y_send, y_recv, r_send, r_recv,
 ):
     gx, gy = lax.axis_index("gx"), lax.axis_index("gy")
@@ -101,8 +106,14 @@
     has_left, has_right = gx > 0, gx < nx - 1
     has_down, has_up = gy > 0, gy < ny - 1
 
-    load = pltpu.make_async_copy(bg_ref, bg_v, load_sem)
-    load.start()
+    loads = [
+        pltpu.make_async_copy(source, target, load_sem.at[i])
+        for i, (source, target) in enumerate((
+            (bg_ref, bg_v), (cells_hbm, cells_ref), (gain_hbm, gain_ref), (cen_hbm, cen_ref), (nei_hbm, nei_ref),
+        ))
+    ]
+    for load in loads:
+        load.start()
 
     barrier = pltpu.get_barrier_semaphore()
     expected = 0
@@ -137,16 +148,21 @@
     sub = lax.broadcasted_iota(jnp.int32, (k, lanes), 0)
     lane = lax.broadcasted_iota(jnp.int32, (k, lanes), 1)
 
+    loads[1].wait()
+    loads[2].wait()
+
     def spread(i, carry):
         cells, gains = carry
         here = sub == i
         return jnp.where(here, cells_ref[i], cells), jnp.where(here, gain_ref[i], gains)
 
-    cells, gains = lax.fori_loop(0, k, spread, (jnp.zeros((k, lanes), jnp.int32), jnp.zeros((k, lanes), F32)))
+    cells, gains = lax.fori_loop(
+        0, k, spread, (jnp.zeros((k, lanes), jnp.int32), jnp.zeros((k, lanes), F32)), unroll=8
+    )
     rel_ref[...] = cells - lane
     gains_ref[...] = gains
 
-    load.wait()
+    loads[0].wait()
 
     def take(i, _):
         x, y = i // width_y, i % width_y
@@ -155,7 +171,7 @@
         v_ref[x + 1, y + 1] = rows + jnp.where(rel_ref[...] == at, gains_ref[...], 0.0)
         return 0
 
-    lax.fori_loop(0, width_x * width_y, take, 0)
+    lax.fori_loop(0, width_x * width_y, take, 0, unroll=8)
     pl.semaphore_wait(barrier, expected + has_left.astype(jnp.int32) + has_right.astype(jnp.int32))
 
     def x_copy(buf, which, c, side):
@@ -224,6 +240,8 @@
         result = result + row(lower) * pltpu.roll(core, 1, 1)
         return result
 
+    loads[3].wait()
+    loads[4].wait()
     arrive_y(v_ref, 0, 0)
     arrive_y(v_ref, 0, 1)
     for c in ROW_CHUNKS:
@@ -234,7 +252,7 @@
             w_ref[x + 1, y + 1] = advance(v_ref, x, y)
             return 0
 
-        lax.fori_loop(0, 2 * width_x, first, 0)
+        lax.fori_loop(0, 2 * width_x, first, 0, unroll=True)
         start_x(w_ref, 1, c)
         if c == 0:
             start_y(w_ref, 1, 0)
@@ -243,7 +261,7 @@
 
     high = jnp.zeros((k, k), F32)
     low = jnp.zeros((k, k), F32)
-    for turn, c in enumerate(ROW_CHUNKS):
+    for c in ROW_CHUNKS:
         arrive_x(w_ref, 1, c)
         if c == 0:
             arrive_y(w_ref, 1, 1)
@@ -256,14 +274,13 @@
             s_ref[c * 2 * width_x + i] = value
             return jnp.maximum(most, jnp.abs(value))
 
-        most = lax.fori_loop(0, 2 * width_x, second, jnp.zeros((k, lanes), F32))
-        part = pl.ds(c * 2 * width_x, 2 * width_x)
-        pltpu.make_async_copy(s_ref.at[part], s_out.at[part], store_sem.at[c]).start()
+        most = lax.fori_loop(0, 2 * width_x, second, jnp.zeros((k, lanes), F32), unroll=True)
         big = power_below(jnp.max(most, axis=1, keepdims=True)) * F32(1.5 * 2**17)
         for i in range(2 * width_x):
             for j, piece in enumerate(pieces(s_ref[c * 2 * width_x + i], big)):
-                xs_ref[turn % 2, j * k : (j + 1) * k, i * lanes : (i + 1) * lanes] = piece.astype(jnp.bfloat16)
-        part_high, part_low = outer_sums(xs_ref[turn % 2])
+                xs_ref[c, j * k : (j + 1) * k, i * lanes : (i + 1) * lanes] = piece.astype(jnp.bfloat16)
+        pltpu.make_async_copy(xs_ref.at[c], xs_out.at[c], store_sem.at[c]).start()
+        part_high, part_low = outer_sums(xs_ref[c])
         high, e = two_sum(high, part_high)
         low = low + (part_low + e)
 
@@ -325,8 +342,7 @@
     for copy in sent:
         copy.wait_send()
     for c in ROW_CHUNKS:
-        part = pl.ds(c * 2 * width_x, 2 * width_x)
-        pltpu.make_async_copy(s_ref.at[part], s_out.at[part], store_sem.at[c]).wait()
+        pltpu.make_async_copy(xs_ref.at[c], xs_out.at[c], store_sem.at[c]).wait()
         for which, buf in enumerate((v_ref, w_ref)):
             for side in (0, 1):
                 @pl.when(there_x[side])
@@ -340,20 +356,38 @@
 
 
 def eliminate(a):
-    n = a.shape[0]
+    n, lanes = a.shape
+    full = (8, lanes)
     blocks = [a[8 * i : 8 * i + 8] for i in range(n // 8)]
-    sub = lax.broadcasted_iota(jnp.int32, (8, 1), 0)
-    for j in range(n):
-        jb, jr = j // 8, j % 8
-        row = blocks[jb][jr : jr + 1]
-        scale = lax.rsqrt(row[:, j : j + 1])
-        row = row * scale
-        for i in range(jb, n // 8):
-            update = (blocks[i][:, j : j + 1] * scale) * row
-            if i == jb:
-                blocks[i] = jnp.where(sub > jr, blocks[i] - update, jnp.where(sub == jr, row, blocks[i]))
-            else:
-                blocks[i] = blocks[i] - update
+    sub = lax.broadcasted_iota(jnp.int32, full, 0)
+    for p in range(n // 8):
+        rest = range(p + 1, n // 8)
+        own = blocks[p]
+
+        def column(block, c, p=p):
+            return jnp.broadcast_to(block[:, 8 * p + c : 8 * p + c + 1], full)
+
+        rows = [jnp.broadcast_to(own[j : j + 1], full) for j in range(8)]
+        own_columns = [column(own, c) for c in range(8)]
+        d = {(i, c): jnp.broadcast_to(own_columns[c][i : i + 1], full) for c in range(8) for i in range(c + 1)}
+        u = {i: [column(blocks[i], c) for c in range(8)] for i in rest}
+        for j in range(8):
+            scale = lax.rsqrt(d[j, j])
+            rows[j] = rows[j] * scale
+            factor = {c: d[j, c] * scale for c in range(j + 1, 8)}
+            for c in range(j + 1, 8):
+                for e in range(c, 8):
+                    d[c, e] = d[c, e] - factor[c] * factor[e]
+                rows[c] = rows[c] - factor[c] * rows[j]
+            for i in rest:
+                u[i][j] = u[i][j] * scale
+                for c in range(j + 1, 8):
+                    u[i][c] = u[i][c] - u[i][j] * factor[c]
+                blocks[i] = blocks[i] - u[i][j] * rows[j]
+        done = rows[0]
+        for j in range(1, 8):
+            done = jnp.where(sub == j, rows[j], done)
+        blocks[p] = done
     return jnp.concatenate(blocks, axis=0)
 
 
@@ -365,9 +399,9 @@
     return jnp.dot(a, b, precision=HIGHEST, preferred_element_type=F32)
 
 
-def basis_kernel(root, s_hbm, g_ref, modes_ref, r_ref, first_ref, s_v, load_sem):
+def basis_kernel(root, xs_hbm, g_ref, modes_ref, r_ref, first_ref, xs_ref, out_ref, load_sem, store_sem):
     k = g_ref.shape[0]
-    load = pltpu.make_async_copy(s_hbm, s_v, load_sem)
+    load = pltpu.make_async_copy(xs_hbm, xs_ref, load_sem)
     load.start()
     high, low = g_ref[:, :k], g_ref[:, k:]
     eye = eye_mask(k, k).astype(F32)
@@ -376,28 +410,32 @@
 
     done = eliminate(jnp.concatenate([high, eye], axis=1))
     first = jnp.where(upper, done[:, :k], 0.0).T
-    big = power_below(jnp.max(jnp.abs(first), axis=1, keepdims=True)) * F32(1.5 * 2**17)
-    parts = [p.astype(jnp.bfloat16) for p in pieces(first, big)]
+    inverse = done[:, k:]
+    parts = cut(first)
     first = (parts[2].astype(F32) + parts[1].astype(F32)) + parts[0].astype(F32)
-    inverse = done[:, k:]
     full, rest = outer_sums(jnp.concatenate(parts, axis=0))
     left = (high - full) + (low - rest)
     gram = eye + dot(dot(inverse, left), inverse.T)
 
     done = eliminate(jnp.concatenate([gram, eye], axis=1))
     second_t = jnp.where(upper, done[:, :k], 0.0)
-    weights = dot(done[:, k:], inverse) * root
+    weights = jnp.concatenate([jnp.concatenate([p] * 3, axis=1) for p in cut(dot(done[:, k:], inverse) * root)], axis=0)
+    load.wait()
+    chunks, lanes = xs_ref.shape[0], out_ref.shape[-1]
+    width_x = out_ref.shape[0]
+    stores = []
+    for x in range(width_x):
+        for c in range(chunks):
+            prod = jnp.dot(weights, xs_ref[c, :, 2 * lanes * x : 2 * lanes * (x + 1)], preferred_element_type=F32)
+            prod = prod[:k] + (prod[k : 2 * k] + prod[2 * k :])
+            for i in range(2):
+                out_ref[x, :, 2 * c + i, :] = prod[:, i * lanes : (i + 1) * lanes]
+        stores.append(pltpu.make_async_copy(out_ref.at[x], modes_ref.at[:, x], store_sem.at[x]))
+        stores[-1].start()
     r_ref[...] = dot(second_t, first.T) * (1.0 / root)
     first_ref[...] = first.T * (1.0 / root)
-    load.wait()
-    count = s_v.shape[0]
-
-    def body(i, _):
-        x, y = i // 2 % (count // 8), i // (count // 4) * 2 + i % 2
-        modes_ref[pl.ds(x * 8 + y, k, stride=count), :] = dot(weights, s_v[i])
-        return 0
-
-    lax.fori_loop(0, count, body, 0)
+    for store in stores:
+        store.wait()
 
 
 def local(nx, ny, background, sensor_cells, sensor_gain, center, neighbours):
@@ -405,34 +443,38 @@
     cells = width_x * width_y
     groups = groups_of(nx)
     vmem = pl.BlockSpec(memory_space=pltpu.VMEM)
-    smem = pl.BlockSpec(memory_space=pltpu.SMEM)
     dma = pltpu.SemaphoreType.DMA
     slots = max([ny] + [g.size for g in groups])
     rows = k // ny
+    pieces_shape = (width_y // 2, 3 * k, 2 * width_x * lanes)
     fields, gram = pl.pallas_call(
         functools.partial(fields_kernel, nx, ny),
-        out_shape=(jax.ShapeDtypeStruct((cells, k, lanes), F32), jax.ShapeDtypeStruct((k, 2 * k), F32)),
-        in_specs=[smem, smem, pl.BlockSpec(memory_space=pl.ANY), vmem, vmem],
-        out_specs=(pl.BlockSpec(memory_space=pl.ANY), vmem),
+        out_shape=(jax.ShapeDtypeStruct(pieces_shape, jnp.bfloat16), jax.ShapeDtypeStruct((k, 2 * k), F32)),
+        in_specs=[pl.BlockSpec(memory_space=pltpu.HBM)] * 5,
+        out_specs=(pl.BlockSpec(memory_space=pltpu.HBM), vmem),
         scratch_shapes=[
+            pltpu.SMEM((k,), jnp.int32),
+            pltpu.SMEM((k,), F32),
+            pltpu.VMEM((cells, lanes), F32),
+            pltpu.VMEM((6, cells, lanes), F32),
             pltpu.VMEM((k * cells, lanes), F32),
             pltpu.VMEM((width_x + 2, width_y + 2, k, lanes), F32),
             pltpu.VMEM((width_x + 2, width_y + 2, k, lanes), F32),
             pltpu.VMEM((cells, k, lanes), F32),
             pltpu.VMEM((k, lanes), jnp.int32),
             pltpu.VMEM((k, lanes), F32),
-            pltpu.VMEM((2, 3 * k, 2 * width_x * lanes), jnp.bfloat16),
+            pltpu.VMEM(pieces_shape, jnp.bfloat16),
             pltpu.VMEM((k, 2 * k), F32),
             pltpu.VMEM((3, rows, 2 * k), F32),
             pltpu.VMEM((ny, rows, 2 * k), F32),
             pltpu.VMEM((groups[0].size, rows, 2 * k), F32),
             pltpu.VMEM((groups[1].size, rows, 2 * k), F32),
-            dma, dma((4,)),
+            dma((5,)), dma((4,)),
             dma((2, 2, 4)), dma((2, 2, 4)), dma((2, 2)), dma((2, 2)),
             dma((4, slots)), dma((4, slots)),
         ],
         compiler_params=pltpu.CompilerParams(
-            collective_id=0, has_side_effects=True, vmem_limit_bytes=24 * 2**20
+            collective_id=0, has_side_effects=True, vmem_limit_bytes=56 * 2**20
         ),
         name="fields_and_products",
     )(
@@ -444,17 +486,19 @@
     modes, r_factor, first_r = pl.pallas_call(
         functools.partial(basis_kernel, root),
         out_shape=(
-            jax.ShapeDtypeStruct((k * cells, lanes), F32),
+            jax.ShapeDtypeStruct(background.shape, F32),
             jax.ShapeDtypeStruct((k, k), F32),
             jax.ShapeDtypeStruct((k, k), F32),
         ),
-        in_specs=[pl.BlockSpec(memory_space=pl.ANY), vmem],
-        out_specs=(vmem, vmem, vmem),
-        scratch_shapes=[pltpu.VMEM((cells, k, lanes), F32), dma],
-        compiler_params=pltpu.CompilerParams(vmem_limit_bytes=24 * 2**20),
+        in_specs=[pl.BlockSpec(memory_space=pltpu.HBM), vmem],
+        out_specs=(pl.BlockSpec(memory_space=pltpu.HBM), vmem, vmem),
+        scratch_shapes=[
+            pltpu.VMEM(pieces_shape, jnp.bfloat16), pltpu.VMEM((width_x, k, width_y, lanes), F32), dma, dma((width_x,)),
+        ],
+        compiler_params=pltpu.CompilerParams(vmem_limit_bytes=56 * 2**20),
         name="basis",
     )(fields, gram)
-    return modes.reshape(background.shape), r_factor, first_r
+    return modes, r_factor, first_r
 
 
 def solution(mesh):

time: 77.6 us -> 62.4 us (0.80)
  Pallas kernels: 73.2 us -> 61.5 us
  local copies, waits for them, and re-layouts: 3.49 us -> 0 us
    pallas_call x1, Pallas kernels: 19.2 us -> 9.38 us  [local(): pl.pallas_call(functools.partial(basis_kernel, root), out_shape=(jax.Shap...]
    unnamed x10 -> x0, local copies, waits for them, and re-layouts: 3.49 us -> none
    pallas_call x1, Pallas kernels: 54 us -> 52.1 us  [local(): pl.pallas_call(functools.partial(fields_kernel, nx, ny), out_shape=(jax.S...]
where the time goes in v2:
time: 62.4 us; the launch traced here: 62.1 us
  Pallas kernels  61.5 us (99%)
  between operations  0.64 us (1%)
    pallas_call x1, Pallas kernels, local(): pl.pallas_call(functools.partial(fields_kernel, nx, ny), out_shape=(jax.S...  52.1 us
    pallas_call x1, Pallas kernels, local(): pl.pallas_call(functools.partial(basis_kernel, root), out_shape=(jax.Shap...  9.38 us

profile of v2, /device:TPU:1, one launch (start us, length us, event | category | flops | bytes accessed | tf_op | source)
XLA Modules:
  0.0 62.1 jit_solution(8893987468465349721)
XLA Ops:
  0.6 52.1 %fields_and_products.1 = (bf16[4,192,1024]{2,1,0:T(8,128)(2,1)}, f32[64,128]{1,0:T(8,128)}) custom-call(s32[64]{0:T(128)} %cells_hbm.1, f32[64]{0:T(128)} %gain_hbm.1, f32[2048,128]{1,0:T(8,128)} %bitcast.3, f32[32,128]{1,0:T(8,128)} %bitcast.5, f32[6,32,128]{2,1,0:T(8,128)} %bitcast.4), custom_call_target="tpu_custom_call" | custom-call | tf_op jit(solution)/shard_map/fields_and_products/pallas_call | solution.py:450
  52.7 9.4 %basis.1 = (f32[64,4,8,128]{3,2,1,0:T(8,128)}, f32[64,64]{1,0:T(8,128)}, f32[64,64]{1,0:T(8,128)}) custom-call(bf16[4,192,1024]{2,1,0:T(8,128)(2,1)} %get-tuple-element.5.xs_hbm, f32[64,128]{1,0:T(8,128)} %get-tuple-element.6.g_ref), custom_call_target="tpu_custom_call" | custom-call | tf_op jit(solution)/shard_map/basis/pallas_call | solution.py:486

commit v3 on v2

--- a/solution.py
+++ b/solution.py
@@ -75,6 +75,22 @@
         return [Group("gx", [(16, 4), (1, 2)]), Group("gx", [(2, 8)])]
     half = size_x // 2
     return [Group("gx", [(1, 2)]), Group("gx", [(2, half)])]
+
+
+class Ring:
+    def __init__(self, axis, stride, count):
+        self.axis, self.stride, self.count = axis, stride, count
+
+    def at(self, distance):
+        me = lax.axis_index(self.axis)
+        digit = (me // self.stride) % self.count
+        steps = sorted({distance % self.count, -distance % self.count} - {0})
+        return [{self.axis: me + ((digit + step) % self.count - digit) * self.stride} for step in steps]
+
+
+def rings_of(nx, ny):
+    deep = 16 if nx == 64 else nx
+    return Ring("gx", 1, deep), Ring("gx", deep, nx // deep), Ring("gy", 2, ny // 2), Ring("gy", 1, 2)
 
 
 def sum_slots(buf, count, lanes):
@@ -97,7 +113,7 @@
 def fields_kernel(
     nx, ny, cells_hbm, gain_hbm, bg_ref, cen_hbm, nei_hbm, xs_out, g_out,
     cells_ref, gain_ref, cen_ref, nei_ref, bg_v, v_ref, w_ref, s_ref, rel_ref, gains_ref, xs_ref, pack_ref, piece_ref, buf0, buf1, buf2,
-    load_sem, store_sem, x_send, x_recv, y_send, y_recv, r_send, r_recv,
+    news_sem, load_sem, store_sem, x_send, x_recv, y_send, y_recv, r_send, r_recv,
 ):
     gx, gy = lax.axis_index("gx"), lax.axis_index("gy")
     width_x, width_y, k, lanes = 4, 8, v_ref.shape[2], v_ref.shape[3]
@@ -116,13 +132,21 @@
         load.start()
 
     barrier = pltpu.get_barrier_semaphore()
-    expected = 0
-    for group in [y_group] + groups:
-        rank = group.rank()
-        for step in range(1, group.size):
-            to = group.member((rank + step) % group.size)
-            pl.semaphore_signal(barrier, inc=1, device_id={group.axis: to}, device_id_type=MESH)
-            expected += 1
+    rings = rings_of(nx, ny)
+    deep = rings[0]
+    near = [to for ring in rings for to in ring.at(1)]
+    rounds = (near, rings[3].at(1) + Ring("gx", 1, 2).at(1) + deep.at(2), deep.at(4))
+    expected = len(near)
+
+    def tell(sem, targets):
+        for to in targets:
+            pl.semaphore_signal(sem, inc=1, device_id=to, device_id_type=MESH)
+
+    def hear(i):
+        if rounds[i]:
+            pl.semaphore_wait(news_sem.at[i], len(rounds[i]))
+
+    tell(barrier, near)
 
     @pl.when(has_left)
     def _():
@@ -131,6 +155,11 @@
     @pl.when(has_right)
     def _():
         pl.semaphore_signal(barrier, inc=1, device_id={"gx": gx + 1}, device_id_type=MESH)
+
+    for there, to in ((has_down, gy - 1), (has_up, gy + 1)):
+        @pl.when(there)
+        def _(to=to):
+            pl.semaphore_signal(barrier, inc=1, device_id={"gy": to}, device_id_type=MESH)
 
     zero_plane = jnp.zeros((width_y, k, lanes), F32)
     for edge, row in ((~has_left, 0), (~has_right, width_x + 1)):
@@ -172,7 +201,9 @@
         return 0
 
     lax.fori_loop(0, width_x * width_y, take, 0, unroll=8)
-    pl.semaphore_wait(barrier, expected + has_left.astype(jnp.int32) + has_right.astype(jnp.int32))
+    for there in (has_left, has_right, has_down, has_up):
+        expected = expected + there.astype(jnp.int32)
+    pl.semaphore_wait(barrier, expected)
 
     def x_copy(buf, which, c, side):
         rows = pl.ds(1 + 2 * c, 2)
@@ -220,6 +251,7 @@
     start_y(v_ref, 0, 1)
     for c in ROW_CHUNKS:
         start_x(v_ref, 0, c)
+    tell(news_sem.at[0], rounds[0])
 
     z_lane = lax.broadcasted_iota(jnp.int32, (1, lanes), 1)
 
@@ -258,6 +290,12 @@
             start_y(w_ref, 1, 0)
         if c == width_y // 2 - 1:
             start_y(w_ref, 1, 1)
+        if c == ROW_CHUNKS[0]:
+            hear(0)
+            tell(news_sem.at[1], rounds[1])
+        if c == ROW_CHUNKS[-1]:
+            hear(1)
+            tell(news_sem.at[2], rounds[2])
 
     high = jnp.zeros((k, k), F32)
     low = jnp.zeros((k, k), F32)
@@ -313,6 +351,7 @@
                 device_id={group.axis: group.member(peer)}, device_id_type=MESH,
             ).wait_recv()
 
+    hear(2)
     sent = []
 
     def part_of(peer):
@@ -469,7 +508,7 @@
             pltpu.VMEM((ny, rows, 2 * k), F32),
             pltpu.VMEM((groups[0].size, rows, 2 * k), F32),
             pltpu.VMEM((groups[1].size, rows, 2 * k), F32),
-            dma((5,)), dma((4,)),
+            pltpu.SemaphoreType.REGULAR((3,)), dma((5,)), dma((4,)),
             dma((2, 2, 4)), dma((2, 2, 4)), dma((2, 2)), dma((2, 2)),
             dma((4, slots)), dma((4, slots)),
         ],

time: 62.4 us -> 59.4 us (0.952)
  Pallas kernels: 61.5 us -> 58.5 us
    pallas_call x1, Pallas kernels: 52.1 us -> 49.1 us  [local(): pl.pallas_call(functools.partial(fields_kernel, nx, ny), out_shape=(jax.S...]
where the time goes in v3:
time: 59.4 us; the launch traced here: 59.2 us
  Pallas kernels  58.5 us (98%)
  between operations  0.64 us (1%)
    pallas_call x1, Pallas kernels, local(): pl.pallas_call(functools.partial(fields_kernel, nx, ny), out_shape=(jax.S...  49.1 us
    pallas_call x1, Pallas kernels, local(): pl.pallas_call(functools.partial(basis_kernel, root), out_shape=(jax.Shap...  9.38 us

profile of v3, /device:TPU:1, one launch (start us, length us, event | category | flops | bytes accessed | tf_op | source)
XLA Modules:
  0.0 59.2 jit_solution(3400782337866909340)
XLA Ops:
  0.6 49.1 %fields_and_products.1 = (bf16[4,192,1024]{2,1,0:T(8,128)(2,1)}, f32[64,128]{1,0:T(8,128)}) custom-call(s32[64]{0:T(128)} %cells_hbm.1, f32[64]{0:T(128)} %gain_hbm.1, f32[2048,128]{1,0:T(8,128)} %bitcast.3, f32[32,128]{1,0:T(8,128)} %bitcast.5, f32[6,32,128]{2,1,0:T(8,128)} %bitcast.4), custom_call_target="tpu_custom_call" | custom-call | tf_op jit(solution)/shard_map/fields_and_products/pallas_call | solution.py:489
  49.8 9.4 %basis.1 = (f32[64,4,8,128]{3,2,1,0:T(8,128)}, f32[64,64]{1,0:T(8,128)}, f32[64,64]{1,0:T(8,128)}) custom-call(bf16[4,192,1024]{2,1,0:T(8,128)(2,1)} %get-tuple-element.5.xs_hbm, f32[64,128]{1,0:T(8,128)} %get-tuple-element.6.g_ref), custom_call_target="tpu_custom_call" | custom-call | tf_op jit(solution)/shard_map/basis/pallas_call | solution.py:525

commit v4 on v3

--- a/solution.py
+++ b/solution.py
@@ -113,7 +113,7 @@
 def fields_kernel(
     nx, ny, cells_hbm, gain_hbm, bg_ref, cen_hbm, nei_hbm, xs_out, g_out,
     cells_ref, gain_ref, cen_ref, nei_ref, bg_v, v_ref, w_ref, s_ref, rel_ref, gains_ref, xs_ref, pack_ref, piece_ref, buf0, buf1, buf2,
-    news_sem, load_sem, store_sem, x_send, x_recv, y_send, y_recv, r_send, r_recv,
+    news_sem, own_sem, load_sem, store_sem, x_send, x_recv, y_send, y_recv, r_send, r_recv,
 ):
     gx, gy = lax.axis_index("gx"), lax.axis_index("gy")
     width_x, width_y, k, lanes = 4, 8, v_ref.shape[2], v_ref.shape[3]
@@ -374,9 +374,11 @@
     def rows_of(r):
         return g_out.at[pl.ds(pl.multiple_of(r * rows, rows), rows)]
 
-    g_out[pl.ds(pl.multiple_of(y_rank * rows, rows), rows)] = total
+    own_rows = pltpu.make_async_copy(last, rows_of(y_rank), own_sem)
+    own_rows.start()
     sent += share(3, y_group, lambda p: last, rows_of, None, None)
     gather(3, y_group, lambda p: last, rows_of)
+    own_rows.wait()
 
     for copy in sent:
         copy.wait_send()
@@ -438,7 +440,7 @@
     return jnp.dot(a, b, precision=HIGHEST, preferred_element_type=F32)
 
 
-def basis_kernel(root, xs_hbm, g_ref, modes_ref, r_ref, first_ref, xs_ref, out_ref, load_sem, store_sem):
+def basis_kernel(root, xs_hbm, g_ref, modes_ref, r_hbm, first_hbm, xs_ref, out_ref, r_ref, first_ref, load_sem, store_sem, small_sem):
     k = g_ref.shape[0]
     load = pltpu.make_async_copy(xs_hbm, xs_ref, load_sem)
     load.start()
@@ -471,9 +473,15 @@
                 out_ref[x, :, 2 * c + i, :] = prod[:, i * lanes : (i + 1) * lanes]
         stores.append(pltpu.make_async_copy(out_ref.at[x], modes_ref.at[:, x], store_sem.at[x]))
         stores[-1].start()
+    small = [
+        pltpu.make_async_copy(source, target, small_sem.at[i])
+        for i, (source, target) in enumerate(((first_ref, first_hbm), (r_ref, r_hbm)))
+    ]
+    first_ref[...] = first.T * (1.0 / root)
+    small[0].start()
     r_ref[...] = dot(second_t, first.T) * (1.0 / root)
-    first_ref[...] = first.T * (1.0 / root)
-    for store in stores:
+    small[1].start()
+    for store in stores + small:
         store.wait()
 
 
@@ -490,7 +498,7 @@
         functools.partial(fields_kernel, nx, ny),
         out_shape=(jax.ShapeDtypeStruct(pieces_shape, jnp.bfloat16), jax.ShapeDtypeStruct((k, 2 * k), F32)),
         in_specs=[pl.BlockSpec(memory_space=pltpu.HBM)] * 5,
-        out_specs=(pl.BlockSpec(memory_space=pltpu.HBM), vmem),
+        out_specs=(pl.BlockSpec(memory_space=pltpu.HBM), pl.BlockSpec(memory_space=pltpu.HBM)),
         scratch_shapes=[
             pltpu.SMEM((k,), jnp.int32),
             pltpu.SMEM((k,), F32),
@@ -508,7 +516,7 @@
             pltpu.VMEM((ny, rows, 2 * k), F32),
             pltpu.VMEM((groups[0].size, rows, 2 * k), F32),
             pltpu.VMEM((groups[1].size, rows, 2 * k), F32),
-            pltpu.SemaphoreType.REGULAR((3,)), dma((5,)), dma((4,)),
+            pltpu.SemaphoreType.REGULAR((3,)), dma, dma((5,)), dma((4,)),
             dma((2, 2, 4)), dma((2, 2, 4)), dma((2, 2)), dma((2, 2)),
             dma((4, slots)), dma((4, slots)),
         ],
@@ -530,9 +538,10 @@
             jax.ShapeDtypeStruct((k, k), F32),
         ),
         in_specs=[pl.BlockSpec(memory_space=pltpu.HBM), vmem],
-        out_specs=(pl.BlockSpec(memory_space=pltpu.HBM), vmem, vmem),
+        out_specs=(pl.BlockSpec(memory_space=pltpu.HBM),) * 3,
         scratch_shapes=[
-            pltpu.VMEM(pieces_shape, jnp.bfloat16), pltpu.VMEM((width_x, k, width_y, lanes), F32), dma, dma((width_x,)),
+            pltpu.VMEM(pieces_shape, jnp.bfloat16), pltpu.VMEM((width_x, k, width_y, lanes), F32),
+            pltpu.VMEM((k, k), F32), pltpu.VMEM((k, k), F32), dma, dma((width_x,)), dma((2,)),
         ],
         compiler_params=pltpu.CompilerParams(vmem_limit_bytes=56 * 2**20),
         name="basis",

time: 59.4 us -> 58.3 us (0.981)
  Pallas kernels: 58.5 us -> 57.4 us
    pallas_call x1, Pallas kernels: 9.38 us -> 8.79 us  [local(): pl.pallas_call(functools.partial(basis_kernel, root), out_shape=(jax.Shap...]
where the time goes in v4:
time: 58.3 us; the launch traced here: 58.1 us
  Pallas kernels  57.4 us (98%)
  between operations  0.64 us (1%)
    pallas_call x1, Pallas kernels, local(): pl.pallas_call(functools.partial(fields_kernel, nx, ny), out_shape=(jax.S...  48.6 us
    pallas_call x1, Pallas kernels, local(): pl.pallas_call(functools.partial(basis_kernel, root), out_shape=(jax.Shap...  8.79 us

profile of v4, /device:TPU:1, one launch (start us, length us, event | category | flops | bytes accessed | tf_op | source)
XLA Modules:
  0.0 58.1 jit_solution(9988462845877402953)
XLA Ops:
  0.6 48.6 %fields_and_products.1 = (bf16[4,192,1024]{2,1,0:T(8,128)(2,1)}, f32[64,128]{1,0:T(8,128)}) custom-call(s32[64]{0:T(128)} %cells_hbm.1, f32[64]{0:T(128)} %gain_hbm.1, f32[2048,128]{1,0:T(8,128)} %bitcast.3, f32[32,128]{1,0:T(8,128)} %bitcast.5, f32[6,32,128]{2,1,0:T(8,128)} %bitcast.4), custom_call_target="tpu_custom_call" | custom-call | tf_op jit(solution)/shard_map/fields_and_products/pallas_call | solution.py:497
  49.3 8.8 %basis.1 = (f32[64,4,8,128]{3,2,1,0:T(8,128)}, f32[64,64]{1,0:T(8,128)}, f32[64,64]{1,0:T(8,128)}) custom-call(bf16[4,192,1024]{2,1,0:T(8,128)(2,1)} %get-tuple-element.5.xs_hbm, f32[64,128]{1,0:T(8,128)} %get-tuple-element.6.g_ref), custom_call_target="tpu_custom_call" | custom-call | tf_op jit(solution)/shard_map/basis/pallas_call | solution.py:533

commit v5 on v4

--- a/solution.py
+++ b/solution.py
@@ -77,6 +77,10 @@
     return [Group("gx", [(1, 2)]), Group("gx", [(2, half)])]
 
 
+def far_first(size):
+    return sorted(range(1, size), key=lambda step: -min(step, size - step))
+
+
 class Ring:
     def __init__(self, axis, stride, count):
         self.axis, self.stride, self.count = axis, stride, count
@@ -94,14 +98,13 @@
 
 
 def sum_slots(buf, count, lanes):
-    def body(i, carry):
-        total, err = carry
-        total, e = two_sum(total, buf[i])
-        return total, err + e
-
-    total, err = buf[0], jnp.zeros_like(buf[0])
-    for i in range(1, count):
-        total, err = body(i, (total, err))
+    totals, err = [buf[i] for i in range(count)], jnp.zeros_like(buf[0])
+    while len(totals) > 1:
+        pairs = [two_sum(a, b) for a, b in zip(totals[::2], totals[1::2])]
+        totals = [total for total, _ in pairs]
+        for _, e in pairs:
+            err = err + e
+    total = totals[0]
     half = lanes // 2
     low = err + pltpu.roll(total, half, 1)
     high = total + low
@@ -330,7 +333,7 @@
     def share(phase, group, source, target, slot, sem_slot):
         rank = group.rank()
         copies = []
-        for step in range(1, group.size):
+        for step in far_first(group.size):
             peer = (rank + step) % group.size
             copies.append(pltpu.make_async_remote_copy(
                 src_ref=source(peer), dst_ref=target(rank),
@@ -463,14 +466,15 @@
     weights = jnp.concatenate([jnp.concatenate([p] * 3, axis=1) for p in cut(dot(done[:, k:], inverse) * root)], axis=0)
     load.wait()
     chunks, lanes = xs_ref.shape[0], out_ref.shape[-1]
-    width_x = out_ref.shape[0]
+    width_x, _, width_y, _ = out_ref.shape
+    flat = out_ref.reshape(width_x, k * width_y, lanes)
     stores = []
     for x in range(width_x):
         for c in range(chunks):
             prod = jnp.dot(weights, xs_ref[c, :, 2 * lanes * x : 2 * lanes * (x + 1)], preferred_element_type=F32)
             prod = prod[:k] + (prod[k : 2 * k] + prod[2 * k :])
             for i in range(2):
-                out_ref[x, :, 2 * c + i, :] = prod[:, i * lanes : (i + 1) * lanes]
+                flat[x, pl.ds(2 * c + i, k, stride=width_y), :] = prod[:, i * lanes : (i + 1) * lanes]
         stores.append(pltpu.make_async_copy(out_ref.at[x], modes_ref.at[:, x], store_sem.at[x]))
         stores[-1].start()
     small = [

time: 58.3 us -> 57.4 us (0.985)
  Pallas kernels: 57.4 us -> 56.5 us
where the time goes in v5:
time: 57.4 us; the launch traced here: 57.2 us
  Pallas kernels  56.5 us (98%)
  between operations  0.64 us (1%)
    pallas_call x1, Pallas kernels, local(): pl.pallas_call(functools.partial(fields_kernel, nx, ny), out_shape=(jax.S...  48.2 us
    pallas_call x1, Pallas kernels, local(): pl.pallas_call(functools.partial(basis_kernel, root), out_shape=(jax.Shap...  8.37 us

profile of v5, /device:TPU:1, one launch (start us, length us, event | category | flops | bytes accessed | tf_op | source)
XLA Modules:
  0.0 57.2 jit_solution(6951233785400431768)
XLA Ops:
  0.6 48.2 %fields_and_products.1 = (bf16[4,192,1024]{2,1,0:T(8,128)(2,1)}, f32[64,128]{1,0:T(8,128)}) custom-call(s32[64]{0:T(128)} %cells_hbm.1, f32[64]{0:T(128)} %gain_hbm.1, f32[2048,128]{1,0:T(8,128)} %bitcast.3, f32[32,128]{1,0:T(8,128)} %bitcast.5, f32[6,32,128]{2,1,0:T(8,128)} %bitcast.4), custom_call_target="tpu_custom_call" | custom-call | tf_op jit(solution)/shard_map/fields_and_products/pallas_call | solution.py:501
  48.8 8.4 %basis.1 = (f32[64,4,8,128]{3,2,1,0:T(8,128)}, f32[64,64]{1,0:T(8,128)}, f32[64,64]{1,0:T(8,128)}) custom-call(bf16[4,192,1024]{2,1,0:T(8,128)(2,1)} %get-tuple-element.5.xs_hbm, f32[64,128]{1,0:T(8,128)} %get-tuple-element.6.g_ref), custom_call_target="tpu_custom_call" | custom-call | tf_op jit(solution)/shard_map/basis/pallas_call | solution.py:537

commit v6 on v5

--- a/solution.py
+++ b/solution.py
@@ -296,7 +296,7 @@
         if c == ROW_CHUNKS[0]:
             hear(0)
             tell(news_sem.at[1], rounds[1])
-        if c == ROW_CHUNKS[-1]:
+        if c == ROW_CHUNKS[-2]:
             hear(1)
             tell(news_sem.at[2], rounds[2])
 
@@ -354,7 +354,6 @@
                 device_id={group.axis: group.member(peer)}, device_id_type=MESH,
             ).wait_recv()
 
-    hear(2)
     sent = []
 
     def part_of(peer):
@@ -365,6 +364,8 @@
     gather(0, y_group, part_of, lambda r: buf0.at[r])
     total = sum_slots(buf0, ny, lanes)
     for phase, (group, buf) in enumerate(zip(groups, (buf1, buf2)), 1):
+        if phase == 2:
+            hear(2)
         here = piece_ref.at[phase - 1]
         here[...] = total
         buf[group.rank()] = total

time: 57.4 us -> 57.4 us (level)
  no operation moved by 1% of the time
where the time goes in v6:
time: 57.4 us; the launch traced here: 57.2 us
  Pallas kernels  56.5 us (98%)
  between operations  0.64 us (1%)
    pallas_call x1, Pallas kernels, local(): pl.pallas_call(functools.partial(fields_kernel, nx, ny), out_shape=(jax.S...  48.2 us
    pallas_call x1, Pallas kernels, local(): pl.pallas_call(functools.partial(basis_kernel, root), out_shape=(jax.Shap...  8.37 us

profile of v6, /device:TPU:1, one launch (start us, length us, event | category | flops | bytes accessed | tf_op | source)
XLA Modules:
  0.0 57.2 jit_solution(3752028362491543723)
XLA Ops:
  0.6 48.2 %fields_and_products.1 = (bf16[4,192,1024]{2,1,0:T(8,128)(2,1)}, f32[64,128]{1,0:T(8,128)}) custom-call(s32[64]{0:T(128)} %cells_hbm.1, f32[64]{0:T(128)} %gain_hbm.1, f32[2048,128]{1,0:T(8,128)} %bitcast.3, f32[32,128]{1,0:T(8,128)} %bitcast.5, f32[6,32,128]{2,1,0:T(8,128)} %bitcast.4), custom_call_target="tpu_custom_call" | custom-call | tf_op jit(solution)/shard_map/fields_and_products/pallas_call | solution.py:502
  48.8 8.4 %basis.1 = (f32[64,4,8,128]{3,2,1,0:T(8,128)}, f32[64,64]{1,0:T(8,128)}, f32[64,64]{1,0:T(8,128)}) custom-call(bf16[4,192,1024]{2,1,0:T(8,128)(2,1)} %get-tuple-element.5.xs_hbm, f32[64,128]{1,0:T(8,128)} %get-tuple-element.6.g_ref), custom_call_target="tpu_custom_call" | custom-call | tf_op jit(solution)/shard_map/basis/pallas_call | solution.py:538
